TPU v7x, 32 devices: a whole 2x2x4 slice. The times are simulated.
32 devices in a mesh: row: 4 (over y, x), col: 8 (over z, core).
Axes of the slice: x: 2, y: 2, z: 4, core: 2. Of those that a mesh axis runs over, the one named last changes fastest.
Arguments:
- excitation: float32 [4, 8, 2, 32, 1024], P('row', 'col'), may hold values from -6 to 6
- shift_real: float32 [4, 8, 1024], P('row', 'col'), may hold values from 6 to 10
- shift_imag: float32 [4, 8, 1024], P('row', 'col'), may hold values from 1.5 to 4
- local_tiles: bfloat16 [4, 8, 8, 4, 128, 128], P('row', 'col'), may hold values from -0.25 to 0.25
- tile_columns: int32 [4, 8, 8, 4], P('row', 'col'), may hold values from 0 to 7
- coupling: bfloat16 [4, 8, 4, 128, 128], P('row', 'col'), may hold values from -0.5 to 0.5
- send_edges: int32 [4, 8, 4, 128], P('row', 'col'), may hold values from 0 to 1023
- receive_edges: int32 [4, 8, 4, 128], P('row', 'col'), may hold values from 0 to 1023
- local_modes: bfloat16 [4, 8, 96, 1024], P('row', 'col'), may hold values from -0.1875 to 0.1875
- coarse_inverse: bfloat16 [3072, 3072], P('row', 'col'), may hold values from -0.15625 to 0.15625
Outputs:
- solution: float32 [4, 8, 2, 32, 1024], P('row', 'col')
- residual: float32 [4, 8, 2, 32, 1024], P('row', 'col')
Inputs may be any that keep to these rules, and one draw needn't show every extreme that they name: `tile_columns`: tile column numbers of one subdomain's operator. `send_edges`: edge numbers within the sending subdomain; an edge may repeat. `receive_edges`: edge numbers within the receiving subdomain; an edge may repeat.
All inputs are finite; a program needn't handle non-finite values.
Results may differ from a plain program's by a relative error of at most 0.0003.
Values sent between devices are 32-bit elements; how exact they have to be, the bound alone decides.
A program may use at most 64 MiB of HBM per device.

v0:
```python
import functools

import jax
import jax.numpy as jnp
from jax import lax
from jax.experimental import pallas as pl
from jax.experimental.pallas import tpu as pltpu
from jax.sharding import PartitionSpec as P

OUTER = 2
PASSES = 2
MESH = pl.DeviceIdType.MESH
NT = (((1,), (1,)), ((), ()))
NN = (((1,), (0,)), ((), ()))


def dot(left, right, dims=NN):
    return lax.dot_general(left, right, dims, preferred_element_type=jnp.float32)


def split(value):
    high = value.astype(jnp.bfloat16)
    low = (value - high.astype(jnp.float32)).astype(jnp.bfloat16)
    return jnp.concatenate([high, low], axis=0)


def fold(value):
    half = value.shape[0] // 2
    return value[:half] + value[half:]


def kernel(
    n_row,
    n_col,
    columns,
    send_list,
    receive_list,
    shift_real,
    shift_imag,
    excitation_hbm,
    tiles_hbm,
    coupling_hbm,
    modes_hbm,
    inverse_hbm,
    solution,
    residual,
    tiles,
    coupling,
    modes,
    inverse,
    picker,
    placer,
    field,
    base,
    coarse_in,
    gathered,
    partial,
    reduced,
    halo_out,
    halo_in,
    load_sem,
    gather_send,
    gather_recv,
    reduce_send,
    reduce_recv,
    halo_send,
    halo_recv,
):
    row = lax.axis_index("row")
    col = lax.axis_index("col")
    sources = residual.shape[0]
    half = sources // 2
    blocks, _, tile = field.shape
    per_row = tiles.shape[1]
    mode_count = modes.shape[0]
    pairs = mode_count // 2
    steps_per_outer = PASSES + 1

    loads = [
        pltpu.make_async_copy(source, target, load_sem.at[number])
        for number, (source, target) in enumerate(
            [
                (excitation_hbm, residual),
                (modes_hbm, modes),
                (inverse_hbm, inverse),
                (tiles_hbm, tiles),
                (coupling_hbm, coupling),
            ]
        )
    ]
    for load in loads:
        load.start()

    barrier = pltpu.get_barrier_semaphore()
    for offset in range(1, n_row):
        pl.semaphore_signal(
            barrier, inc=1, device_id={"row": lax.rem(row + offset, n_row)}, device_id_type=MESH
        )
    for offset in range(1, n_col):
        pl.semaphore_signal(
            barrier, inc=1, device_id={"col": lax.rem(col + offset, n_col)}, device_id_type=MESH
        )

    directions = picker.shape[1] // tile
    edge = lax.broadcasted_iota(jnp.int32, (blocks * tile, tile), 0)
    for d in range(directions):
        lanes = slice(d * tile, (d + 1) * tile)
        picker[:, lanes] = (edge == send_list[d : d + 1, :]).astype(jnp.bfloat16)
        placer[:, lanes] = (edge == receive_list[d : d + 1, :]).astype(jnp.bfloat16)
    solution[...] = jnp.zeros_like(solution)

    exists = [row > 0, row < n_row - 1, col > 0, col < n_col - 1]
    target = [{"row": row - 1}, {"row": row + 1}, {"col": col - 1}, {"col": col + 1}]

    for d in range(directions):

        @pl.when(jnp.logical_not(exists[d]))
        def _():
            for k in range(halo_in.shape[0]):
                halo_in[k, d] = jnp.zeros(halo_in.shape[2:], jnp.float32)

    for load in loads:
        load.wait()
    pl.semaphore_wait(barrier, n_row - 1 + n_col - 1)

    lane = lax.broadcasted_iota(jnp.int32, (pairs, 2 * sources), 1)
    first = lane < sources

    def packed(value):
        top, bottom = value[:pairs], value[pairs:]
        other = jnp.where(first, bottom, top)
        return jnp.where(first, top, bottom) + pltpu.roll(other, sources, 1)

    def unpacked(value):
        turned = pltpu.roll(value, sources, 1)
        return jnp.concatenate(
            [jnp.where(first, value, turned), jnp.where(first, turned, value)], axis=0
        )

    def gather_copy(step, offset, slot):
        return pltpu.make_async_remote_copy(
            src_ref=gathered.at[step, slot],
            dst_ref=gathered.at[step, slot],
            send_sem=gather_send.at[step, offset - 1],
            recv_sem=gather_recv.at[step, slot],
            device_id={"row": lax.rem(row + offset, n_row)},
            device_id_type=MESH,
        )

    def reduce_copy(step, offset):
        peer = lax.rem(col + offset, n_col)
        return pltpu.make_async_remote_copy(
            src_ref=partial.at[step, peer],
            dst_ref=reduced.at[step, offset - 1],
            send_sem=reduce_send.at[step, offset - 1],
            recv_sem=reduce_recv.at[step, offset - 1],
            device_id={"col": peer},
            device_id_type=MESH,
        )

    def halo_copy(k, d):
        return pltpu.make_async_remote_copy(
            src_ref=halo_out.at[k, d],
            dst_ref=halo_in.at[k, d ^ 1],
            send_sem=halo_send.at[k, d],
            recv_sem=halo_recv.at[k, d ^ 1],
            device_id=target[d],
            device_id_type=MESH,
        )

    def halo_arrival(k, d):
        return pltpu.make_async_remote_copy(
            src_ref=halo_out.at[k, d],
            dst_ref=halo_in.at[k, d],
            send_sem=halo_send.at[k, d],
            recv_sem=halo_recv.at[k, d],
            device_id=target[d],
            device_id_type=MESH,
        )

    def keep_field(value):
        parts = split(value)
        for b in range(blocks):
            field[b] = parts[:, b * tile : (b + 1) * tile]

    def coarse(step):
        projected = dot(modes[...], split(residual[...]), NT)
        gathered[step, row] = packed(projected)
        for offset in range(1, n_row):
            gather_copy(step, offset, row).start()
        for offset in range(1, n_row):
            gather_copy(step, offset, lax.rem(row + offset, n_row)).wait_recv()
        low_part = lax.broadcasted_iota(jnp.int32, (mode_count, 2 * sources), 1) >= sources
        for i in range(n_row):
            value = unpacked(gathered[step, i])
            high = value.astype(jnp.bfloat16).astype(jnp.float32)
            coarse_in[i * mode_count : (i + 1) * mode_count, :] = jnp.where(
                low_part, value - high, high
            ).astype(jnp.bfloat16)
        for offset in list(range(1, n_col)) + [0]:
            peer = lax.rem(col + offset, n_col)
            partial[step, peer] = packed(dot(inverse[peer], coarse_in[...]))
            if offset:
                reduce_copy(step, offset).start()
        total = partial[step, col]
        for offset in range(1, n_col):
            reduce_copy(step, offset).wait_recv()
            total = total + reduced[step, offset - 1]
        columns_of = unpacked(total)
        padding = jnp.zeros((2 * sources - mode_count, 2 * sources), jnp.float32)
        turned = jnp.concatenate([columns_of, padding], axis=0).T[:sources, :mode_count]
        start = fold(dot(split(turned), modes[...]))
        keep_field(start)
        solution[...] += start
        real, imag = shift_real[...], shift_imag[...]
        base[:half] = residual[:half] - (real * start[:half] - imag * start[half:])
        base[half:] = residual[half:] - (real * start[half:] + imag * start[:half])
        for offset in range(1, n_row):
            gather_copy(step, offset, row).wait_send()
        for offset in range(1, n_col):
            reduce_copy(step, offset).wait_send()

    def body(k, carry):
        step = lax.div(k, steps_per_outer)
        sub = lax.rem(k, steps_per_outer)

        @pl.when(sub == 0)
        def _():
            coarse(step)

        whole = jnp.concatenate([field[b] for b in range(blocks)], axis=1)
        outgoing = fold(dot(whole, picker[...]))
        for d in range(directions):
            halo_out[k, d] = outgoing[:, d * tile : (d + 1) * tile]

            @pl.when(exists[d])
            def _():
                halo_copy(k, d).start()

        for t in range(tiles.shape[0]):
            chosen = jnp.concatenate([field[columns[t, n]] for n in range(per_row)], axis=1)
            stored = jnp.concatenate([tiles[t, n] for n in range(per_row)], axis=1)
            lanes = slice(t * tile, (t + 1) * tile)
            residual[:, lanes] = base[:, lanes] - fold(dot(chosen, stored, NT))

        arrived = []
        for d in range(directions):

            @pl.when(exists[d])
            def _():
                halo_arrival(k, d).wait_recv()

            arrived.append(split(fold(dot(split(halo_in[k, d]), coupling[d], NT))))
        moved = jnp.concatenate(arrived, axis=1)
        result = residual[...] - fold(dot(moved, placer[...], NT))
        residual[...] = result

        @pl.when(sub < PASSES)
        def _():
            real, imag = shift_real[...], shift_imag[...]
            modulus = real * real + imag * imag
            real, imag = real / modulus, imag / modulus
            relaxed = jnp.concatenate(
                [
                    real * result[:half] + imag * result[half:],
                    real * result[half:] - imag * result[:half],
                ],
                axis=0,
            )
            keep_field(relaxed)
            solution[...] += relaxed
            base[...] = jnp.zeros_like(base)

        for d in range(directions):

            @pl.when(exists[d])
            def _():
                halo_copy(k, d).wait_send()

        return carry

    lax.fori_loop(0, OUTER * steps_per_outer, body, 0)


def on_device(
    n_row,
    n_col,
    excitation,
    shift_real,
    shift_imag,
    local_tiles,
    tile_columns,
    coupling,
    send_edges,
    receive_edges,
    local_modes,
    coarse_inverse,
):
    shape = excitation.shape
    edges = shape[-1]
    sources = shape[2] * shape[3]
    tile_rows, per_row, tile, _ = local_tiles.shape[2:]
    directions = send_edges.shape[2]
    mode_count = local_modes.shape[2]
    applies = OUTER * (PASSES + 1)
    vmem = pl.BlockSpec(memory_space=pltpu.VMEM)
    hbm = pl.BlockSpec(memory_space=pl.ANY)
    flat = jax.ShapeDtypeStruct((sources, edges), jnp.float32)
    inverse = coarse_inverse.reshape(n_col, mode_count, coarse_inverse.shape[1])
    results = pl.pallas_call(
        functools.partial(kernel, n_row, n_col),
        out_shape=(flat, flat),
        in_specs=[pl.BlockSpec(memory_space=pltpu.SMEM)] + [vmem] * 4 + [hbm] * 5,
        out_specs=(vmem, vmem),
        scratch_shapes=[
            pltpu.VMEM(local_tiles.shape[2:], jnp.bfloat16),
            pltpu.VMEM(coupling.shape[2:], jnp.bfloat16),
            pltpu.VMEM(local_modes.shape[2:], jnp.bfloat16),
            pltpu.VMEM(inverse.shape, jnp.bfloat16),
            pltpu.VMEM((edges, directions * tile), jnp.bfloat16),
            pltpu.VMEM((edges, directions * tile), jnp.bfloat16),
            pltpu.VMEM((edges // tile, 2 * sources, tile), jnp.bfloat16),
            pltpu.VMEM((sources, edges), jnp.float32),
            pltpu.VMEM((n_row * mode_count, 2 * sources), jnp.bfloat16),
            pltpu.VMEM((OUTER, n_row, mode_count // 2, 2 * sources), jnp.float32),
            pltpu.VMEM((OUTER, n_col, mode_count // 2, 2 * sources), jnp.float32),
            pltpu.VMEM((OUTER, n_col - 1, mode_count // 2, 2 * sources), jnp.float32),
            pltpu.VMEM((applies, directions, sources, tile), jnp.float32),
            pltpu.VMEM((applies, directions, sources, tile), jnp.float32),
            pltpu.SemaphoreType.DMA((5,)),
            pltpu.SemaphoreType.DMA((OUTER, n_row - 1)),
            pltpu.SemaphoreType.DMA((OUTER, n_row)),
            pltpu.SemaphoreType.DMA((OUTER, n_col - 1)),
            pltpu.SemaphoreType.DMA((OUTER, n_col - 1)),
            pltpu.SemaphoreType.DMA((applies, directions)),
            pltpu.SemaphoreType.DMA((applies, directions)),
        ],
        compiler_params=pltpu.CompilerParams(
            collective_id=0, has_side_effects=True, vmem_limit_bytes=40 * 1024 * 1024
        ),
    )(
        tile_columns[0, 0],
        send_edges[0, 0],
        receive_edges[0, 0],
        shift_real[0],
        shift_imag[0],
        excitation.reshape(sources, edges),
        local_tiles[0, 0],
        coupling[0, 0],
        local_modes[0, 0],
        inverse,
    )
    return tuple(value.reshape(shape) for value in results)


def solution(mesh):
    in_specs = (
        P("row", "col", None, None, None),
        P("row", "col", None),
        P("row", "col", None),
        P("row", "col", None, None, None, None),
        P("row", "col", None, None),
        P("row", "col", None, None, None),
        P("row", "col", None, None),
        P("row", "col", None, None),
        P("row", "col", None, None),
        P("row", "col"),
    )
    out_specs = (P("row", "col", None, None, None), P("row", "col", None, None, None))
    return jax.shard_map(
        functools.partial(on_device, mesh.shape["row"], mesh.shape["col"]),
        mesh=mesh,
        in_specs=in_specs,
        out_specs=out_specs,
        check_vma=False,
    )
```

profile of v0, /device:TPU:0, one launch (start us, length us, event | category | flops | bytes accessed | tf_op | source)
XLA Modules:
  0.0 63.0 jit_solution(17174194485051038679)
XLA Ops:
  0.6 0.0 copy-start.9
  0.6 0.0 copy-start.8
  0.7 0.0 copy-start.7
  0.7 0.0 copy-start.6
  0.7 0.0 copy-start.5
  0.7 0.6 %copy-done.9 = s32[1,1,8,4]{2,3,1,0:T(4,128)S(1)} copy-done((s32[1,1,8,4]{2,3,1,0:T(4,128)S(1)}, s32[1,1,8,4]{2,3,1,0:T(4,128)}, u32[]{:S(2)}) %copy-start.9) | copy-done | bytes 152
  1.3 0.1 copy.12.columns
  1.4 0.0 copy-done.8
  1.4 0.0 copy-done.7
  1.4 0.0 copy-done.6
  1.4 0.0 copy-done.5
  1.4 0.0 copy-start
  1.4 1.2 %copy-done = bf16[1,1,8,4,128,128]{5,4,3,2,1,0:T(8,128)(2,1)S(1)} copy-done((bf16[1,1,8,4,128,128]{5,4,3,2,1,0:T(8,128)(2,1)S(1)}, bf16[1,1,8,4,128,128]{5,4,3,2,1,0:T(8,128)(2,1)}, u32[]{:S(2)}) %copy-start) | copy-done | bytes 1048600
  2.6 0.0 copy-start.1
  2.6 1.1 %copy-done.1 = bf16[768,384]{1,0:T(8,128)(2,1)S(1)} copy-done((bf16[768,384]{1,0:T(8,128)(2,1)S(1)}, bf16[768,384]{1,0:T(8,128)(2,1)}, u32[]{:S(2)}) %copy-start.1) | copy-done | bytes 589848
  3.7 0.0 copy-start.2
  3.7 0.9 %copy-done.2 = f32[1,1,2,32,1024]{4,3,2,1,0:T(8,128)S(1)} copy-done((f32[1,1,2,32,1024]{4,3,2,1,0:T(8,128)S(1)}, f32[1,1,2,32,1024]{4,3,2,1,0:T(8,128)}, u32[]{:S(2)}) %copy-start.2) | copy-done | bytes 262168
  4.7 0.0 copy-start.3
  4.7 0.9 %copy-done.3 = bf16[1,1,96,1024]{3,2,1,0:T(8,128)(2,1)S(1)} copy-done((bf16[1,1,96,1024]{3,2,1,0:T(8,128)(2,1)S(1)}, bf16[1,1,96,1024]{3,2,1,0:T(8,128)(2,1)}, u32[]{:S(2)}) %copy-start.3) | copy-done | bytes 196632
  5.6 0.0 copy-start.4
  5.6 0.9 %copy-done.4 = bf16[1,1,4,128,128]{4,3,2,1,0:T(8,128)(2,1)S(1)} copy-done((bf16[1,1,4,128,128]{4,3,2,1,0:T(8,128)(2,1)S(1)}, bf16[1,1,4,128,128]{4,3,2,1,0:T(8,128)(2,1)}, u32[]{:S(2)}) %copy-start.4) | copy-done | bytes 131096
  6.5 55.1 %shard_map.113 = (f32[64,1024]{1,0:T(8,128)S(1)}, f32[64,1024]{1,0:T(8,128)S(1)}) custom-call(s32[8,4]{1,0:T(8,128)S(1)} %copy.12.columns, s32[4,128]{1,0:T(4,128)S(1)} %bitcast.21, s32[4,128]{1,0:T(4,128)S(1)} %bitcast.22, f32[1,1024]{1,0:T(1,128)S(1)} %bitcast.19, f32[1,1024]{1,0:T(1,128)S(1)} %bitcast.20, f32[64,1024]{1,0:T(8,128)S(1)} %bitcast.14, ...), custom_call_target="tpu_custom_call" | custom-call | tf_op jit(solution)/shard_map/pallas_call | solution.py:310
  61.5 0.7 %copy.15 = f32[1,1,2,32,1024]{4,3,2,1,0:T(8,128)} copy(f32[1,1,2,32,1024]{4,3,2,1,0:T(8,128)S(1)} %bitcast.16) | data formatting | bytes 524288
  62.2 0.7 %copy.16 = f32[1,1,2,32,1024]{4,3,2,1,0:T(8,128)} copy(f32[1,1,2,32,1024]{4,3,2,1,0:T(8,128)S(1)} %bitcast.15) | data formatting | bytes 524288
Async XLA Ops:
  0.6 0.7 %copy-start.9 = (s32[1,1,8,4]{2,3,1,0:T(4,128)S(1)}, s32[1,1,8,4]{2,3,1,0:T(4,128)}, u32[]{:S(2)}) copy-start(s32[1,1,8,4]{2,3,1,0:T(4,128)} %param.14) | copy-start | bytes 388
  0.6 0.8 %copy-start.8 = (s32[1,1,4,128]{3,2,1,0:T(4,128)S(1)}, s32[1,1,4,128]{3,2,1,0:T(4,128)}, u32[]{:S(2)}) copy-start(s32[1,1,4,128]{3,2,1,0:T(4,128)} %param.17) | copy-start | bytes 6148
  0.7 0.7 %copy-start.7 = (s32[1,1,4,128]{3,2,1,0:T(4,128)S(1)}, s32[1,1,4,128]{3,2,1,0:T(4,128)}, u32[]{:S(2)}) copy-start(s32[1,1,4,128]{3,2,1,0:T(4,128)} %param.16) | copy-start | bytes 6148
  0.7 0.7 %copy-start.6 = (f32[1,1,1024]{2,1,0:T(1,128)S(1)}, f32[1,1,1024]{2,1,0:T(1,128)}, u32[]{:S(2)}) copy-start(f32[1,1,1024]{2,1,0:T(1,128)} %param.12) | copy-start | bytes 12292
  0.7 0.7 %copy-start.5 = (f32[1,1,1024]{2,1,0:T(1,128)S(1)}, f32[1,1,1024]{2,1,0:T(1,128)}, u32[]{:S(2)}) copy-start(f32[1,1,1024]{2,1,0:T(1,128)} %param.11) | copy-start | bytes 12292
  1.4 1.2 %copy-start = (bf16[1,1,8,4,128,128]{5,4,3,2,1,0:T(8,128)(2,1)S(1)}, bf16[1,1,8,4,128,128]{5,4,3,2,1,0:T(8,128)(2,1)}, u32[]{:S(2)}) copy-start(bf16[1,1,8,4,128,128]{5,4,3,2,1,0:T(8,128)(2,1)} %param.13) | copy-start | bytes 3145732
  2.6 1.1 %copy-start.1 = (bf16[768,384]{1,0:T(8,128)(2,1)S(1)}, bf16[768,384]{1,0:T(8,128)(2,1)}, u32[]{:S(2)}) copy-start(bf16[768,384]{1,0:T(8,128)(2,1)} %param.19) | copy-start | bytes 1769476
  3.7 0.9 %copy-start.2 = (f32[1,1,2,32,1024]{4,3,2,1,0:T(8,128)S(1)}, f32[1,1,2,32,1024]{4,3,2,1,0:T(8,128)}, u32[]{:S(2)}) copy-start(f32[1,1,2,32,1024]{4,3,2,1,0:T(8,128)} %param.10) | copy-start | bytes 786436
  4.7 0.9 %copy-start.3 = (bf16[1,1,96,1024]{3,2,1,0:T(8,128)(2,1)S(1)}, bf16[1,1,96,1024]{3,2,1,0:T(8,128)(2,1)}, u32[]{:S(2)}) copy-start(bf16[1,1,96,1024]{3,2,1,0:T(8,128)(2,1)} %param.18) | copy-start | bytes 589828
  5.6 0.9 %copy-start.4 = (bf16[1,1,4,128,128]{4,3,2,1,0:T(8,128)(2,1)S(1)}, bf16[1,1,4,128,128]{4,3,2,1,0:T(8,128)(2,1)}, u32[]{:S(2)}) copy-start(bf16[1,1,4,128,128]{4,3,2,1,0:T(8,128)(2,1)} %param.15) | copy-start | bytes 393220
where the time goes:
time: 63.3 us; the launch traced here: 63 us
  Pallas kernels  55.1 us (87%)
  local copies, waits for them, and re-layouts  7.2 us (11%)
  between operations  0.7 us (1%)
    pallas_call x1, Pallas kernels, on_device(): pl.pallas_call(functools.partial(kernel, n_row, n_col), out_shape=(flat,...  55.1 us
    unnamed x22, local copies, waits for them, and re-layouts  7.12 us

commit v1 on v0

--- a/solution.py
+++ b/solution.py
@@ -102,11 +102,6 @@
         )
 
     directions = picker.shape[1] // tile
-    edge = lax.broadcasted_iota(jnp.int32, (blocks * tile, tile), 0)
-    for d in range(directions):
-        lanes = slice(d * tile, (d + 1) * tile)
-        picker[:, lanes] = (edge == send_list[d : d + 1, :]).astype(jnp.bfloat16)
-        placer[:, lanes] = (edge == receive_list[d : d + 1, :]).astype(jnp.bfloat16)
     solution[...] = jnp.zeros_like(solution)
 
     exists = [row > 0, row < n_row - 1, col > 0, col < n_col - 1]
@@ -119,7 +114,7 @@
             for k in range(halo_in.shape[0]):
                 halo_in[k, d] = jnp.zeros(halo_in.shape[2:], jnp.float32)
 
-    for load in loads:
+    for load in loads[:2]:
         load.wait()
     pl.semaphore_wait(barrier, n_row - 1 + n_col - 1)
 
@@ -183,11 +178,42 @@
         for b in range(blocks):
             field[b] = parts[:, b * tile : (b + 1) * tile]
 
+    def prepare_edges():
+        edge = lax.broadcasted_iota(jnp.int32, (blocks * tile, tile), 0)
+        along = lax.broadcasted_iota(jnp.int32, (tile, tile), 1)
+        for d in range(directions):
+            part = slice(d * tile, (d + 1) * tile)
+            picker[:, part] = (edge == send_list[d : d + 1, :]).astype(jnp.bfloat16)
+            receiver = jnp.broadcast_to(receive_list[d : d + 1, :], (tile, tile)).T
+            for b in range(blocks):
+                placer[part, b * tile : (b + 1) * tile] = (receiver == along + b * tile).astype(
+                    jnp.bfloat16
+                )
+
+    def prepare_tiles():
+        for load in loads[3:]:
+            load.wait()
+
+        def turn(t, carry):
+            for n in range(per_row):
+                tiles[t, n] = tiles[t, n].T
+            return carry
+
+        lax.fori_loop(0, tiles.shape[0], turn, 0)
+        for d in range(directions):
+            coupling[d] = coupling[d].T
+
     def coarse(step):
         projected = dot(modes[...], split(residual[...]), NT)
         gathered[step, row] = packed(projected)
         for offset in range(1, n_row):
             gather_copy(step, offset, row).start()
+
+        @pl.when(step == 0)
+        def _():
+            prepare_edges()
+            loads[2].wait()
+
         for offset in range(1, n_row):
             gather_copy(step, offset, lax.rem(row + offset, n_row)).wait_recv()
         low_part = lax.broadcasted_iota(jnp.int32, (mode_count, 2 * sources), 1) >= sources
@@ -197,11 +223,17 @@
             coarse_in[i * mode_count : (i + 1) * mode_count, :] = jnp.where(
                 low_part, value - high, high
             ).astype(jnp.bfloat16)
-        for offset in list(range(1, n_col)) + [0]:
+        far_first = sorted(range(1, n_col), key=lambda offset: abs(2 * offset - n_col))
+        for offset in far_first + [0]:
             peer = lax.rem(col + offset, n_col)
             partial[step, peer] = packed(dot(inverse[peer], coarse_in[...]))
             if offset:
                 reduce_copy(step, offset).start()
+
+        @pl.when(step == 0)
+        def _():
+            prepare_tiles()
+
         total = partial[step, col]
         for offset in range(1, n_col):
             reduce_copy(step, offset).wait_recv()
@@ -229,30 +261,34 @@
             coarse(step)
 
         whole = jnp.concatenate([field[b] for b in range(blocks)], axis=1)
-        outgoing = fold(dot(whole, picker[...]))
-        for d in range(directions):
-            halo_out[k, d] = outgoing[:, d * tile : (d + 1) * tile]
-
-            @pl.when(exists[d])
-            def _():
-                halo_copy(k, d).start()
+        pairs_of = [range(d, d + 2) for d in range(0, directions, 2)]
+        for group in pairs_of:
+            span = slice(group[0] * tile, (group[-1] + 1) * tile)
+            outgoing = fold(dot(whole, picker[:, span]))
+            for place, d in enumerate(group):
+                halo_out[k, d] = outgoing[:, place * tile : (place + 1) * tile]
+
+                @pl.when(exists[d])
+                def _():
+                    halo_copy(k, d).start()
 
         for t in range(tiles.shape[0]):
-            chosen = jnp.concatenate([field[columns[t, n]] for n in range(per_row)], axis=1)
-            stored = jnp.concatenate([tiles[t, n] for n in range(per_row)], axis=1)
+            chosen = jnp.concatenate([field[columns[n, t]] for n in range(per_row)], axis=1)
+            stored = jnp.concatenate([tiles[t, n] for n in range(per_row)], axis=0)
             lanes = slice(t * tile, (t + 1) * tile)
-            residual[:, lanes] = base[:, lanes] - fold(dot(chosen, stored, NT))
-
-        arrived = []
-        for d in range(directions):
-
-            @pl.when(exists[d])
-            def _():
-                halo_arrival(k, d).wait_recv()
-
-            arrived.append(split(fold(dot(split(halo_in[k, d]), coupling[d], NT))))
-        moved = jnp.concatenate(arrived, axis=1)
-        result = residual[...] - fold(dot(moved, placer[...], NT))
+            residual[:, lanes] = base[:, lanes] - fold(dot(chosen, stored))
+
+        result = residual[...]
+        for group in reversed(pairs_of):
+            span = slice(group[0] * tile, (group[-1] + 1) * tile)
+            for d in group:
+
+                @pl.when(exists[d])
+                def _():
+                    halo_arrival(k, d).wait_recv()
+
+            arrived = [split(fold(dot(split(halo_in[k, d]), coupling[d]))) for d in group]
+            result = result - fold(dot(jnp.concatenate(arrived, axis=1), placer[span, :]))
         residual[...] = result
 
         @pl.when(sub < PASSES)
@@ -318,7 +354,7 @@
             pltpu.VMEM(local_modes.shape[2:], jnp.bfloat16),
             pltpu.VMEM(inverse.shape, jnp.bfloat16),
             pltpu.VMEM((edges, directions * tile), jnp.bfloat16),
-            pltpu.VMEM((edges, directions * tile), jnp.bfloat16),
+            pltpu.VMEM((directions * tile, edges), jnp.bfloat16),
             pltpu.VMEM((edges // tile, 2 * sources, tile), jnp.bfloat16),
             pltpu.VMEM((sources, edges), jnp.float32),
             pltpu.VMEM((n_row * mode_count, 2 * sources), jnp.bfloat16),
@@ -336,10 +372,10 @@
             pltpu.SemaphoreType.DMA((applies, directions)),
         ],
         compiler_params=pltpu.CompilerParams(
-            collective_id=0, has_side_effects=True, vmem_limit_bytes=40 * 1024 * 1024
+            collective_id=0, has_side_effects=True, vmem_limit_bytes=63 * 1024 * 1024
         ),
     )(
-        tile_columns[0, 0],
+        tile_columns[0, 0].T,
         send_edges[0, 0],
         receive_edges[0, 0],
         shift_real[0],

time: 63.3 us -> 55.5 us (0.88)
  local copies, waits for them, and re-layouts: 7.2 us -> 2.42 us
  Pallas kernels: 55.1 us -> 52.2 us
    unnamed x22 -> x4, local copies, waits for them, and re-layouts: 7.12 us -> 2.42 us
    pallas_call x1, Pallas kernels: 55.1 us -> 52.2 us  [on_device(): pl.pallas_call(functools.partial(kernel, n_row, n_col), out_shape=(flat,...]
where the time goes in v1:
time: 55.5 us; the launch traced here: 55.3 us
  Pallas kernels  52.2 us (94%)
  local copies, waits for them, and re-layouts  2.42 us (4%)
  between operations  0.65 us (1%)
    pallas_call x1, Pallas kernels, on_device(): pl.pallas_call(functools.partial(kernel, n_row, n_col), out_shape=(flat,...  52.2 us
    unnamed x4, local copies, waits for them, and re-layouts  2.42 us

profile of v1, /device:TPU:0, one launch (start us, length us, event | category | flops | bytes accessed | tf_op | source)
XLA Modules:
  0.0 55.3 jit_solution(15463675525833240900)
XLA Ops:
  0.6 52.2 %shard_map.113 = (f32[64,1024]{1,0:T(8,128)}, f32[64,1024]{1,0:T(8,128)}) custom-call(s32[4,8]{1,0:T(4,128)} %bitcast.23, s32[4,128]{1,0:T(4,128)} %bitcast.24, s32[4,128]{1,0:T(4,128)} %bitcast.25, f32[1,1024]{1,0:T(1,128)} %bitcast.21, f32[1,1024]{1,0:T(1,128)} %bitcast.22, f32[64,1024]{1,0:T(8,128)} %bitcast.16, bf16[8,4,128,128]{3,2,1,0:T(8,128)(2,1)} %bitcast.14, ...), custom_call_target="tpu_custom_call" | custom-call | tf_op jit(solution)/shard_map/pallas_call | solution.py:346
  52.9 0.0 copy-start
  52.9 1.7 %copy.14 = f32[1,1,2,32,1024]{4,3,2,1,0:T(8,128)} copy(f32[1,1,2,32,1024]{4,3,2,1,0:T(8,128)} %bitcast.18) | data formatting | bytes 524288
  54.6 0.0 copy-done
  54.6 0.7 %copy.15 = f32[1,1,2,32,1024]{4,3,2,1,0:T(8,128)} copy(f32[1,1,2,32,1024]{4,3,2,1,0:T(8,128)S(1)} %bitcast.17) | data formatting | bytes 524288
Async XLA Ops:
  52.9 1.7 %copy-start = (f32[64,1024]{1,0:T(8,128)S(1)}, f32[64,1024]{1,0:T(8,128)}, u32[]{:S(2)}) copy-start(f32[64,1024]{1,0:T(8,128)} %get-tuple-element.5) | copy-start | bytes 786436

commit v2 on v1

--- a/solution.py
+++ b/solution.py
@@ -55,12 +55,15 @@
     coarse_in,
     gathered,
     partial,
+    shared,
     reduced,
     halo_out,
     halo_in,
     load_sem,
     gather_send,
     gather_recv,
+    pair_send,
+    pair_recv,
     reduce_send,
     reduce_recv,
     halo_send,
@@ -114,10 +117,6 @@
             for k in range(halo_in.shape[0]):
                 halo_in[k, d] = jnp.zeros(halo_in.shape[2:], jnp.float32)
 
-    for load in loads[:2]:
-        load.wait()
-    pl.semaphore_wait(barrier, n_row - 1 + n_col - 1)
-
     lane = lax.broadcasted_iota(jnp.int32, (pairs, 2 * sources), 1)
     first = lane < sources
 
@@ -142,14 +141,27 @@
             device_id_type=MESH,
         )
 
+    count = n_col // 2
+    pair, member = lax.div(col, 2), lax.rem(col, 2)
+    far_first = sorted(range(1, count), key=lambda offset: abs(2 * offset - count)) + [0]
+
+    def pair_copy(step, offset):
+        return pltpu.make_async_remote_copy(
+            src_ref=partial.at[step, offset, 0],
+            dst_ref=shared.at[step, offset],
+            send_sem=pair_send.at[step, offset],
+            recv_sem=pair_recv.at[step, offset],
+            device_id={"col": 2 * pair + 1 - member},
+            device_id_type=MESH,
+        )
+
     def reduce_copy(step, offset):
-        peer = lax.rem(col + offset, n_col)
         return pltpu.make_async_remote_copy(
-            src_ref=partial.at[step, peer],
+            src_ref=partial.at[step, offset, 1],
             dst_ref=reduced.at[step, offset - 1],
             send_sem=reduce_send.at[step, offset - 1],
             recv_sem=reduce_recv.at[step, offset - 1],
-            device_id={"col": peer},
+            device_id={"col": 2 * lax.rem(pair + offset, count) + member},
             device_id_type=MESH,
         )
 
@@ -177,6 +189,14 @@
         parts = split(value)
         for b in range(blocks):
             field[b] = parts[:, b * tile : (b + 1) * tile]
+
+    def project(step):
+        gathered[step, row] = packed(dot(modes[...], split(residual[...]), NT))
+
+    for load in loads[:2]:
+        load.wait()
+    project(0)
+    pl.semaphore_wait(barrier, n_row - 1 + n_col - 1)
 
     def prepare_edges():
         edge = lax.broadcasted_iota(jnp.int32, (blocks * tile, tile), 0)
@@ -204,8 +224,6 @@
             coupling[d] = coupling[d].T
 
     def coarse(step):
-        projected = dot(modes[...], split(residual[...]), NT)
-        gathered[step, row] = packed(projected)
         for offset in range(1, n_row):
             gather_copy(step, offset, row).start()
 
@@ -223,10 +241,15 @@
             coarse_in[i * mode_count : (i + 1) * mode_count, :] = jnp.where(
                 low_part, value - high, high
             ).astype(jnp.bfloat16)
-        far_first = sorted(range(1, n_col), key=lambda offset: abs(2 * offset - n_col))
-        for offset in far_first + [0]:
-            peer = lax.rem(col + offset, n_col)
-            partial[step, peer] = packed(dot(inverse[peer], coarse_in[...]))
+        for offset in far_first:
+            start = 2 * lax.rem(pair + offset, count)
+            partial[step, offset, 0] = packed(dot(inverse[start + 1 - member], coarse_in[...]))
+            pair_copy(step, offset).start()
+        for offset in far_first:
+            start = 2 * lax.rem(pair + offset, count)
+            own = packed(dot(inverse[start + member], coarse_in[...]))
+            pair_copy(step, offset).wait_recv()
+            partial[step, offset, 1] = own + shared[step, offset]
             if offset:
                 reduce_copy(step, offset).start()
 
@@ -234,8 +257,8 @@
         def _():
             prepare_tiles()
 
-        total = partial[step, col]
-        for offset in range(1, n_col):
+        total = partial[step, 0, 1]
+        for offset in range(1, count):
             reduce_copy(step, offset).wait_recv()
             total = total + reduced[step, offset - 1]
         columns_of = unpacked(total)
@@ -249,8 +272,10 @@
         base[half:] = residual[half:] - (real * start[half:] + imag * start[:half])
         for offset in range(1, n_row):
             gather_copy(step, offset, row).wait_send()
-        for offset in range(1, n_col):
+        for offset in range(1, count):
             reduce_copy(step, offset).wait_send()
+        for offset in range(count):
+            pair_copy(step, offset).wait_send()
 
     def body(k, carry):
         step = lax.div(k, steps_per_outer)
@@ -306,6 +331,10 @@
             keep_field(relaxed)
             solution[...] += relaxed
             base[...] = jnp.zeros_like(base)
+
+        @pl.when(jnp.logical_and(sub == PASSES, step < OUTER - 1))
+        def _():
+            project(step + 1)
 
         for d in range(directions):
 
@@ -359,15 +388,18 @@
             pltpu.VMEM((sources, edges), jnp.float32),
             pltpu.VMEM((n_row * mode_count, 2 * sources), jnp.bfloat16),
             pltpu.VMEM((OUTER, n_row, mode_count // 2, 2 * sources), jnp.float32),
-            pltpu.VMEM((OUTER, n_col, mode_count // 2, 2 * sources), jnp.float32),
-            pltpu.VMEM((OUTER, n_col - 1, mode_count // 2, 2 * sources), jnp.float32),
+            pltpu.VMEM((OUTER, n_col // 2, 2, mode_count // 2, 2 * sources), jnp.float32),
+            pltpu.VMEM((OUTER, n_col // 2, mode_count // 2, 2 * sources), jnp.float32),
+            pltpu.VMEM((OUTER, n_col // 2 - 1, mode_count // 2, 2 * sources), jnp.float32),
             pltpu.VMEM((applies, directions, sources, tile), jnp.float32),
             pltpu.VMEM((applies, directions, sources, tile), jnp.float32),
             pltpu.SemaphoreType.DMA((5,)),
             pltpu.SemaphoreType.DMA((OUTER, n_row - 1)),
             pltpu.SemaphoreType.DMA((OUTER, n_row)),
-            pltpu.SemaphoreType.DMA((OUTER, n_col - 1)),
-            pltpu.SemaphoreType.DMA((OUTER, n_col - 1)),
+            pltpu.SemaphoreType.DMA((OUTER, n_col // 2)),
+            pltpu.SemaphoreType.DMA((OUTER, n_col // 2)),
+            pltpu.SemaphoreType.DMA((OUTER, n_col // 2 - 1)),
+            pltpu.SemaphoreType.DMA((OUTER, n_col // 2 - 1)),
             pltpu.SemaphoreType.DMA((applies, directions)),
             pltpu.SemaphoreType.DMA((applies, directions)),
         ],

time: 55.5 us -> 56.1 us (1.011)
  Pallas kernels: 52.2 us -> 52.8 us
    pallas_call x1, Pallas kernels: 52.2 us -> 52.8 us  [on_device(): pl.pallas_call(functools.partial(kernel, n_row, n_col), out_shape=(flat,...]
where the time goes in v2:
time: 56.1 us; the launch traced here: 55.9 us
  Pallas kernels  52.8 us (94%)
  local copies, waits for them, and re-layouts  2.42 us (4%)
  between operations  0.65 us (1%)
    pallas_call x1, Pallas kernels, on_device(): pl.pallas_call(functools.partial(kernel, n_row, n_col), out_shape=(flat,...  52.8 us
    unnamed x4, local copies, waits for them, and re-layouts  2.42 us

profile of v2, /device:TPU:0, one launch (start us, length us, event | category | flops | bytes accessed | tf_op | source)
XLA Modules:
  0.0 55.9 jit_solution(11717141691322117370)
XLA Ops:
  0.6 52.8 %shard_map.113 = (f32[64,1024]{1,0:T(8,128)}, f32[64,1024]{1,0:T(8,128)}) custom-call(s32[4,8]{1,0:T(4,128)} %bitcast.23, s32[4,128]{1,0:T(4,128)} %bitcast.24, s32[4,128]{1,0:T(4,128)} %bitcast.25, f32[1,1024]{1,0:T(1,128)} %bitcast.21, f32[1,1024]{1,0:T(1,128)} %bitcast.22, f32[64,1024]{1,0:T(8,128)} %bitcast.16, bf16[8,4,128,128]{3,2,1,0:T(8,128)(2,1)} %bitcast.14, ...), custom_call_target="tpu_custom_call" | custom-call | tf_op jit(solution)/shard_map/pallas_call | solution.py:375
  53.4 0.0 copy-start
  53.4 1.7 %copy.14 = f32[1,1,2,32,1024]{4,3,2,1,0:T(8,128)} copy(f32[1,1,2,32,1024]{4,3,2,1,0:T(8,128)} %bitcast.18) | data formatting | bytes 524288
  55.2 0.0 copy-done
  55.2 0.7 %copy.15 = f32[1,1,2,32,1024]{4,3,2,1,0:T(8,128)} copy(f32[1,1,2,32,1024]{4,3,2,1,0:T(8,128)S(1)} %bitcast.17) | data formatting | bytes 524288
Async XLA Ops:
  53.4 1.7 %copy-start = (f32[64,1024]{1,0:T(8,128)S(1)}, f32[64,1024]{1,0:T(8,128)}, u32[]{:S(2)}) copy-start(f32[64,1024]{1,0:T(8,128)} %get-tuple-element.5) | copy-start | bytes 786436

commit v3 on v1

--- a/solution.py
+++ b/solution.py
@@ -114,10 +114,6 @@
             for k in range(halo_in.shape[0]):
                 halo_in[k, d] = jnp.zeros(halo_in.shape[2:], jnp.float32)
 
-    for load in loads[:2]:
-        load.wait()
-    pl.semaphore_wait(barrier, n_row - 1 + n_col - 1)
-
     lane = lax.broadcasted_iota(jnp.int32, (pairs, 2 * sources), 1)
     first = lane < sources
 
@@ -178,17 +174,34 @@
         for b in range(blocks):
             field[b] = parts[:, b * tile : (b + 1) * tile]
 
+    def project(step):
+        gathered[step, row] = packed(dot(modes[...], split(residual[...]), NT))
+
+    for load in loads[:2]:
+        load.wait()
+    project(0)
+    pl.semaphore_wait(barrier, n_row - 1 + n_col - 1)
+
     def prepare_edges():
-        edge = lax.broadcasted_iota(jnp.int32, (blocks * tile, tile), 0)
         along = lax.broadcasted_iota(jnp.int32, (tile, tile), 1)
-        for d in range(directions):
-            part = slice(d * tile, (d + 1) * tile)
-            picker[:, part] = (edge == send_list[d : d + 1, :]).astype(jnp.bfloat16)
-            receiver = jnp.broadcast_to(receive_list[d : d + 1, :], (tile, tile)).T
-            for b in range(blocks):
-                placer[part, b * tile : (b + 1) * tile] = (receiver == along + b * tile).astype(
+        down = lax.broadcasted_iota(jnp.int32, (tile, tile), 0)
+        receivers = [
+            jnp.broadcast_to(receive_list[d : d + 1, :], (tile, tile)).T for d in range(directions)
+        ]
+
+        def one_block(b, carry):
+            start = pl.multiple_of(b * tile, tile)
+            for d in range(directions):
+                part = slice(d * tile, (d + 1) * tile)
+                picker[pl.ds(start, tile), part] = (
+                    down + start == send_list[d : d + 1, :]
+                ).astype(jnp.bfloat16)
+                placer[part, pl.ds(start, tile)] = (receivers[d] == along + start).astype(
                     jnp.bfloat16
                 )
+            return carry
+
+        lax.fori_loop(0, blocks, one_block, 0)
 
     def prepare_tiles():
         for load in loads[3:]:
@@ -204,8 +217,6 @@
             coupling[d] = coupling[d].T
 
     def coarse(step):
-        projected = dot(modes[...], split(residual[...]), NT)
-        gathered[step, row] = packed(projected)
         for offset in range(1, n_row):
             gather_copy(step, offset, row).start()
 
@@ -223,12 +234,11 @@
             coarse_in[i * mode_count : (i + 1) * mode_count, :] = jnp.where(
                 low_part, value - high, high
             ).astype(jnp.bfloat16)
-        far_first = sorted(range(1, n_col), key=lambda offset: abs(2 * offset - n_col))
-        for offset in far_first + [0]:
-            peer = lax.rem(col + offset, n_col)
-            partial[step, peer] = packed(dot(inverse[peer], coarse_in[...]))
-            if offset:
-                reduce_copy(step, offset).start()
+        products = dot(inverse[...].reshape(n_col * mode_count, -1), coarse_in[...])
+        for j in range(n_col):
+            partial[step, j] = packed(products[j * mode_count : (j + 1) * mode_count])
+        for offset in sorted(range(1, n_col), key=lambda offset: abs(2 * offset - n_col)):
+            reduce_copy(step, offset).start()
 
         @pl.when(step == 0)
         def _():
@@ -272,11 +282,14 @@
                 def _():
                     halo_copy(k, d).start()
 
-        for t in range(tiles.shape[0]):
+        def local(t, carry):
             chosen = jnp.concatenate([field[columns[n, t]] for n in range(per_row)], axis=1)
-            stored = jnp.concatenate([tiles[t, n] for n in range(per_row)], axis=0)
-            lanes = slice(t * tile, (t + 1) * tile)
+            stored = tiles[t].reshape(per_row * tile, tile)
+            lanes = pl.ds(pl.multiple_of(t * tile, tile), tile)
             residual[:, lanes] = base[:, lanes] - fold(dot(chosen, stored))
+            return carry
+
+        lax.fori_loop(0, tiles.shape[0], local, 0)
 
         result = residual[...]
         for group in reversed(pairs_of):
@@ -306,6 +319,10 @@
             keep_field(relaxed)
             solution[...] += relaxed
             base[...] = jnp.zeros_like(base)
+
+        @pl.when(jnp.logical_and(sub == PASSES, step < OUTER - 1))
+        def _():
+            project(step + 1)
 
         for d in range(directions):
 

time: 55.5 us -> 55.5 us (level)
  no operation moved by 1% of the time
where the time goes in v3:
time: 55.5 us; the launch traced here: 55.3 us
  Pallas kernels  52.2 us (94%)
  local copies, waits for them, and re-layouts  2.42 us (4%)
  between operations  0.65 us (1%)
    pallas_call x1, Pallas kernels, on_device(): pl.pallas_call(functools.partial(kernel, n_row, n_col), out_shape=(flat,...  52.2 us
    unnamed x4, local copies, waits for them, and re-layouts  2.42 us

profile of v3, /device:TPU:0, one launch (start us, length us, event | category | flops | bytes accessed | tf_op | source)
XLA Modules:
  0.0 55.3 jit_solution(4020022636239922816)
XLA Ops:
  0.6 52.2 %shard_map.113 = (f32[64,1024]{1,0:T(8,128)}, f32[64,1024]{1,0:T(8,128)}) custom-call(s32[4,8]{1,0:T(4,128)} %bitcast.23, s32[4,128]{1,0:T(4,128)} %bitcast.24, s32[4,128]{1,0:T(4,128)} %bitcast.25, f32[1,1024]{1,0:T(1,128)} %bitcast.21, f32[1,1024]{1,0:T(1,128)} %bitcast.22, f32[64,1024]{1,0:T(8,128)} %bitcast.16, bf16[8,4,128,128]{3,2,1,0:T(8,128)(2,1)} %bitcast.14, ...), custom_call_target="tpu_custom_call" | custom-call | tf_op jit(solution)/shard_map/pallas_call | solution.py:363
  52.9 0.0 copy-start
  52.9 1.7 %copy.14 = f32[1,1,2,32,1024]{4,3,2,1,0:T(8,128)} copy(f32[1,1,2,32,1024]{4,3,2,1,0:T(8,128)} %bitcast.18) | data formatting | bytes 524288
  54.6 0.0 copy-done
  54.6 0.7 %copy.15 = f32[1,1,2,32,1024]{4,3,2,1,0:T(8,128)} copy(f32[1,1,2,32,1024]{4,3,2,1,0:T(8,128)S(1)} %bitcast.17) | data formatting | bytes 524288
Async XLA Ops:
  52.9 1.7 %copy-start = (f32[64,1024]{1,0:T(8,128)S(1)}, f32[64,1024]{1,0:T(8,128)}, u32[]{:S(2)}) copy-start(f32[64,1024]{1,0:T(8,128)} %get-tuple-element.5) | copy-start | bytes 786436

commit v4 on v3

v4 whole, which is shorter than its diff:
```python
import functools

import jax
import jax.numpy as jnp
from jax import lax
from jax.experimental import pallas as pl
from jax.experimental.pallas import tpu as pltpu
from jax.sharding import PartitionSpec as P

OUTER = 2
PASSES = 2
GROUPS = 2
MESH = pl.DeviceIdType.MESH
NT = (((1,), (1,)), ((), ()))
NN = (((1,), (0,)), ((), ()))


def dot(left, right, dims=NN):
    return lax.dot_general(left, right, dims, preferred_element_type=jnp.float32)


def split(value):
    high = value.astype(jnp.bfloat16)
    low = (value - high.astype(jnp.float32)).astype(jnp.bfloat16)
    return jnp.concatenate([high, low], axis=0)


def fold(value):
    half = value.shape[0] // 2
    return value[:half] + value[half:]


def kernel(
    n_row,
    n_col,
    columns,
    send_list,
    receive_list,
    shift_real,
    shift_imag,
    excitation_hbm,
    tiles_hbm,
    coupling_hbm,
    modes_hbm,
    inverse_hbm,
    solution_hbm,
    residual_hbm,
    solution,
    residual,
    tiles,
    coupling,
    modes,
    modes_turned,
    inverse,
    inverse_turned,
    picker,
    placer,
    field,
    base,
    gathered,
    partial,
    reduced,
    halo_out,
    halo_in,
    load_sem,
    store_sem,
    gather_send,
    gather_recv,
    reduce_send,
    reduce_recv,
    halo_send,
    halo_recv,
):
    row = lax.axis_index("row")
    col = lax.axis_index("col")
    groups, sources, _ = residual.shape
    half = sources // 2
    _, blocks, _, tile = field.shape
    per_row = tiles.shape[1]
    directions = halo_in.shape[2]
    applies = halo_in.shape[0]
    mode_count = modes_hbm.shape[0]
    padded = modes.shape[0]
    steps_per_outer = PASSES + 1

    def state_copies(source, target, sems, reverse):
        copies = []
        for g in range(groups):
            for p in range(2):
                whole = source.at[p, pl.ds(g * half, half), :]
                part = target.at[g, pl.ds(p * half, half), :]
                first, second = (part, whole) if reverse else (whole, part)
                copies.append(pltpu.make_async_copy(first, second, sems.at[2 * g + p]))
        return copies

    early = state_copies(excitation_hbm, residual, load_sem, False)
    number = len(early)
    early.append(
        pltpu.make_async_copy(modes_hbm, modes.at[pl.ds(0, mode_count), :], load_sem.at[number])
    )
    late = [
        pltpu.make_async_copy(source, target, load_sem.at[number + 1 + place])
        for place, (source, target) in enumerate(
            [(inverse_hbm, inverse), (tiles_hbm, tiles), (coupling_hbm, coupling)]
        )
    ]
    for load in early + late:
        load.start()

    barrier = pltpu.get_barrier_semaphore()
    for offset in range(1, n_row):
        pl.semaphore_signal(
            barrier, inc=1, device_id={"row": lax.rem(row + offset, n_row)}, device_id_type=MESH
        )
    for offset in range(1, n_col):
        pl.semaphore_signal(
            barrier, inc=1, device_id={"col": lax.rem(col + offset, n_col)}, device_id_type=MESH
        )

    exists = [row > 0, row < n_row - 1, col > 0, col < n_col - 1]
    target = [{"row": row - 1}, {"row": row + 1}, {"col": col - 1}, {"col": col + 1}]

    solution[...] = jnp.zeros_like(solution)
    modes[mode_count:, :] = jnp.zeros((padded - mode_count, modes.shape[1]), jnp.bfloat16)
    for d in range(directions):

        @pl.when(jnp.logical_not(exists[d]))
        def _():
            for k in range(applies):
                for g in range(groups):
                    halo_in[k, g, d] = jnp.zeros(halo_in.shape[3:], jnp.float32)

    def gather_copy(step, g, offset, slot):
        return pltpu.make_async_remote_copy(
            src_ref=gathered.at[step, g, slot],
            dst_ref=gathered.at[step, g, slot],
            send_sem=gather_send.at[step, g, offset - 1],
            recv_sem=gather_recv.at[step, g, slot],
            device_id={"row": lax.rem(row + offset, n_row)},
            device_id_type=MESH,
        )

    def reduce_copy(step, g, offset):
        peer = lax.rem(col + offset, n_col)
        return pltpu.make_async_remote_copy(
            src_ref=partial.at[step, g, peer],
            dst_ref=reduced.at[step, g, offset - 1],
            send_sem=reduce_send.at[step, g, offset - 1],
            recv_sem=reduce_recv.at[step, g, offset - 1],
            device_id={"col": peer},
            device_id_type=MESH,
        )

    def halo_copy(k, g, d, slot):
        return pltpu.make_async_remote_copy(
            src_ref=halo_out.at[k, g, d],
            dst_ref=halo_in.at[k, g, slot],
            send_sem=halo_send.at[k, g, d],
            recv_sem=halo_recv.at[k, g, slot],
            device_id=target[d],
            device_id_type=MESH,
        )

    def gather_start(step, g):
        for offset in range(1, n_row):
            gather_copy(step, g, offset, row).start()

    for load in early:
        load.wait()
    for g in range(groups):
        gathered[0, g, row] = fold(dot(split(residual[g]), modes[...], NT))
    pl.semaphore_wait(barrier, n_row - 1 + n_col - 1)
    for g in range(groups):
        gather_start(0, g)

    def prepare_first():
        late[0].wait()
        blank = jnp.zeros((padded - mode_count, inverse.shape[2]), jnp.bfloat16)

        def turn(j, carry):
            block = jnp.concatenate([inverse[j], blank], axis=0).T
            inverse_turned[:, pl.ds(pl.multiple_of(j * padded, padded), padded)] = block
            return carry

        lax.fori_loop(0, n_col, turn, 0)

    def prepare_edges():
        along = lax.broadcasted_iota(jnp.int32, (tile, tile), 1)
        down = lax.broadcasted_iota(jnp.int32, (tile, tile), 0)
        receivers = [
            jnp.broadcast_to(receive_list[d : d + 1, :], (tile, tile)).T for d in range(directions)
        ]

        def one_block(b, carry):
            start = pl.multiple_of(b * tile, tile)
            for d in range(directions):
                part = slice(d * tile, (d + 1) * tile)
                picker[pl.ds(start, tile), part] = (
                    down + start == send_list[d : d + 1, :]
                ).astype(jnp.bfloat16)
                placer[part, pl.ds(start, tile)] = (receivers[d] == along + start).astype(
                    jnp.bfloat16
                )
            return carry

        lax.fori_loop(0, blocks, one_block, 0)

    def prepare_rest():
        for load in late[1:]:
            load.wait()

        def turn(t, carry):
            for n in range(per_row):
                tiles[t, n] = tiles[t, n].T
            return carry

        lax.fori_loop(0, tiles.shape[0], turn, 0)
        for d in range(directions):
            coupling[d] = coupling[d].T
        for b in range(blocks):
            part = slice(b * tile, (b + 1) * tile)
            modes_turned[part, :] = modes[:, part].T

    def send_field(k, g, value):
        parts = split(value)
        for b in range(blocks):
            field[g, b] = parts[:, b * tile : (b + 1) * tile]
        for first in range(0, directions, 2):
            outgoing = fold(dot(parts, picker[:, first * tile : (first + 2) * tile]))
            for d in (first, first + 1):
                halo_out[k, g, d] = outgoing[:, (d - first) * tile : (d - first + 1) * tile]

                @pl.when(exists[d])
                def _():
                    halo_copy(k, g, d, d ^ 1).start()

    def coarse_product(step, g):
        for offset in range(1, n_row):
            gather_copy(step, g, offset, lax.rem(row + offset, n_row)).wait_recv()
        whole = jnp.concatenate(
            [gathered[step, g, i][:, :mode_count] for i in range(n_row)], axis=1
        )
        products = fold(dot(split(whole), inverse_turned[...]))
        for j in range(n_col):
            partial[step, g, j] = products[:, j * padded : (j + 1) * padded]
        for offset in sorted(range(1, n_col), key=lambda offset: abs(2 * offset - n_col)):
            reduce_copy(step, g, offset).start()

    def coarse_start(step, k, g):
        total = partial[step, g, col]
        for offset in range(1, n_col):
            reduce_copy(step, g, offset).wait_recv()
            total = total + reduced[step, g, offset - 1]
        start = fold(dot(split(total), modes[...]))
        send_field(k, g, start)
        solution[g] += start
        real, imag = shift_real[...], shift_imag[...]
        old = residual[g]
        base[g, :half] = old[:half] - (real * start[:half] - imag * start[half:])
        base[g, half:] = old[half:] - (real * start[half:] + imag * start[:half])

    def apply(step, sub, k, g):
        def local(t, carry):
            chosen = jnp.concatenate([field[g, columns[n, t]] for n in range(per_row)], axis=1)
            stored = tiles[t].reshape(per_row * tile, tile)
            lanes = pl.ds(pl.multiple_of(t * tile, tile), tile)
            residual[g, :, lanes] = base[g, :, lanes] - fold(dot(chosen, stored))
            return carry

        lax.fori_loop(0, tiles.shape[0], local, 0, unroll=2)

        result = residual[g]
        for first in range(directions - 2, -1, -2):
            arrived = []
            for d in (first, first + 1):

                @pl.when(exists[d])
                def _():
                    halo_copy(k, g, d, d).wait_recv()

            for d in (first, first + 1):
                arrived.append(split(fold(dot(split(halo_in[k, g, d]), coupling[d]))))
            span = slice(first * tile, (first + 2) * tile)
            result = result - fold(dot(jnp.concatenate(arrived, axis=1), placer[span, :]))
        residual[g] = result

        @pl.when(sub < PASSES)
        def _():
            real, imag = shift_real[...], shift_imag[...]
            modulus = real * real + imag * imag
            real, imag = real / modulus, imag / modulus
            relaxed = jnp.concatenate(
                [
                    real * result[:half] + imag * result[half:],
                    real * result[half:] - imag * result[:half],
                ],
                axis=0,
            )
            send_field(k + 1, g, relaxed)
            solution[g] += relaxed
            base[g] = jnp.zeros(base.shape[1:], jnp.float32)

        @pl.when(jnp.logical_and(sub == PASSES, step < OUTER - 1))
        def _():
            gathered[step + 1, g, row] = fold(dot(split(result), modes_turned[...]))
            gather_start(step + 1, g)

    def each_group(action):
        def run(g, carry):
            action(g)
            return carry

        lax.fori_loop(0, groups, run, 0)

    def body(k, carry):
        step = lax.div(k, steps_per_outer)
        sub = lax.rem(k, steps_per_outer)

        @pl.when(k == 0)
        def _():
            prepare_first()
            prepare_edges()

        @pl.when(sub == 0)
        def _():
            each_group(lambda g: coarse_product(step, g))

        @pl.when(k == 0)
        def _():
            prepare_rest()

        @pl.when(sub == 0)
        def _():
            each_group(lambda g: coarse_start(step, k, g))

        each_group(lambda g: apply(step, sub, k, g))
        return carry

    lax.fori_loop(0, applies, body, 0)

    stores = state_copies(residual_hbm, residual, store_sem.at[0], True)
    stores += state_copies(solution_hbm, solution, store_sem.at[1], True)
    for store in stores:
        store.start()

    def finish(g):
        for step in range(OUTER):
            for offset in range(1, n_row):
                gather_copy(step, g, offset, row).wait_send()
            for offset in range(1, n_col):
                reduce_copy(step, g, offset).wait_send()
        for d in range(directions):

            @pl.when(exists[d])
            def _():
                for k in range(applies):
                    halo_copy(k, g, d, d ^ 1).wait_send()

    each_group(finish)
    for store in stores:
        store.wait()


def on_device(
    n_row,
    n_col,
    excitation,
    shift_real,
    shift_imag,
    local_tiles,
    tile_columns,
    coupling,
    send_edges,
    receive_edges,
    local_modes,
    coarse_inverse,
):
    shape = excitation.shape
    edges = shape[-1]
    sources = shape[2] * shape[3] // GROUPS
    tile_rows, per_row, tile, _ = local_tiles.shape[2:]
    directions = send_edges.shape[2]
    mode_count = local_modes.shape[2]
    padded = -(-mode_count // tile) * tile
    applies = OUTER * (PASSES + 1)
    vmem = pl.BlockSpec(memory_space=pltpu.VMEM)
    hbm = pl.BlockSpec(memory_space=pl.ANY)
    flat = jax.ShapeDtypeStruct(shape[2:], jnp.float32)
    state = pltpu.VMEM((GROUPS, sources, edges), jnp.float32)
    halo = pltpu.VMEM((applies, GROUPS, directions, sources, tile), jnp.float32)
    inverse = coarse_inverse.reshape(n_col, mode_count, coarse_inverse.shape[1])
    results = pl.pallas_call(
        functools.partial(kernel, n_row, n_col),
        out_shape=(flat, flat),
        in_specs=[pl.BlockSpec(memory_space=pltpu.SMEM)] + [vmem] * 4 + [hbm] * 5,
        out_specs=(hbm, hbm),
        scratch_shapes=[
            state,
            state,
            pltpu.VMEM(local_tiles.shape[2:], jnp.bfloat16),
            pltpu.VMEM(coupling.shape[2:], jnp.bfloat16),
            pltpu.VMEM((padded, edges), jnp.bfloat16),
            pltpu.VMEM((edges, padded), jnp.bfloat16),
            pltpu.VMEM(inverse.shape, jnp.bfloat16),
            pltpu.VMEM((inverse.shape[2], n_col * padded), jnp.bfloat16),
            pltpu.VMEM((edges, directions * tile), jnp.bfloat16),
            pltpu.VMEM((directions * tile, edges), jnp.bfloat16),
            pltpu.VMEM((GROUPS, edges // tile, 2 * sources, tile), jnp.bfloat16),
            state,
            pltpu.VMEM((OUTER, GROUPS, n_row, sources, padded), jnp.float32),
            pltpu.VMEM((OUTER, GROUPS, n_col, sources, padded), jnp.float32),
            pltpu.VMEM((OUTER, GROUPS, n_col - 1, sources, padded), jnp.float32),
            halo,
            halo,
            pltpu.SemaphoreType.DMA((2 * GROUPS + 4,)),
            pltpu.SemaphoreType.DMA((2, 2 * GROUPS)),
            pltpu.SemaphoreType.DMA((OUTER, GROUPS, n_row - 1)),
            pltpu.SemaphoreType.DMA((OUTER, GROUPS, n_row)),
            pltpu.SemaphoreType.DMA((OUTER, GROUPS, n_col - 1)),
            pltpu.SemaphoreType.DMA((OUTER, GROUPS, n_col - 1)),
            pltpu.SemaphoreType.DMA((applies, GROUPS, directions)),
            pltpu.SemaphoreType.DMA((applies, GROUPS, directions)),
        ],
        compiler_params=pltpu.CompilerParams(
            collective_id=0, has_side_effects=True, vmem_limit_bytes=63 * 1024 * 1024
        ),
    )(
        tile_columns[0, 0].T,
        send_edges[0, 0],
        receive_edges[0, 0],
        shift_real[0],
        shift_imag[0],
        excitation[0, 0],
        local_tiles[0, 0],
        coupling[0, 0],
        local_modes[0, 0],
        inverse,
    )
    return tuple(value.reshape(shape) for value in results)


def solution(mesh):
    in_specs = (
        P("row", "col", None, None, None),
        P("row", "col", None),
        P("row", "col", None),
        P("row", "col", None, None, None, None),
        P("row", "col", None, None),
        P("row", "col", None, None, None),
        P("row", "col", None, None),
        P("row", "col", None, None),
        P("row", "col", None, None),
        P("row", "col"),
    )
    out_specs = (P("row", "col", None, None, None), P("row", "col", None, None, None))
    return jax.shard_map(
        functools.partial(on_device, mesh.shape["row"], mesh.shape["col"]),
        mesh=mesh,
        in_specs=in_specs,
        out_specs=out_specs,
        check_vma=False,
    )
```

time: 55.5 us -> 55.3 us (level)
  Pallas kernels: 52.2 us -> 51.6 us
    pallas_call x1, Pallas kernels: 52.2 us -> 51.6 us  [on_device(): pl.pallas_call(functools.partial(kernel, n_row, n_col), out_shape=(flat,...]
where the time goes in v4:
time: 55.3 us; the launch traced here: 54.7 us
  Pallas kernels  51.6 us (93%)
  local copies, waits for them, and re-layouts  2.42 us (4%)
  between operations  0.65 us (1%)
    pallas_call x1, Pallas kernels, on_device(): pl.pallas_call(functools.partial(kernel, n_row, n_col), out_shape=(flat,...  51.6 us
    unnamed x4, local copies, waits for them, and re-layouts  2.42 us

profile of v4, /device:TPU:0, one launch (start us, length us, event | category | flops | bytes accessed | tf_op | source)
XLA Modules:
  0.0 54.7 jit_solution(9594194879305392886)
XLA Ops:
  0.6 51.6 %shard_map.113 = (f32[2,32,1024]{2,1,0:T(8,128)}, f32[2,32,1024]{2,1,0:T(8,128)}) custom-call(s32[4,8]{1,0:T(4,128)} %bitcast.23, s32[4,128]{1,0:T(4,128)} %bitcast.24, s32[4,128]{1,0:T(4,128)} %bitcast.25, f32[1,1024]{1,0:T(1,128)} %bitcast.21, f32[1,1024]{1,0:T(1,128)} %bitcast.22, f32[2,32,1024]{2,1,0:T(8,128)} %bitcast.16, ...), custom_call_target="tpu_custom_call" | custom-call | tf_op jit(solution)/shard_map/pallas_call | solution.py:392
  52.3 0.0 copy-start
  52.3 1.7 %copy.14 = f32[1,1,2,32,1024]{4,3,2,1,0:T(8,128)} copy(f32[1,1,2,32,1024]{4,3,2,1,0:T(8,128)} %bitcast.18) | data formatting | bytes 524288
  54.0 0.0 copy-done
  54.0 0.7 %copy.15 = f32[1,1,2,32,1024]{4,3,2,1,0:T(8,128)} copy(f32[1,1,2,32,1024]{4,3,2,1,0:T(8,128)S(1)} %bitcast.17) | data formatting | bytes 524288
Async XLA Ops:
  52.3 1.7 %copy-start = (f32[2,32,1024]{2,1,0:T(8,128)S(1)}, f32[2,32,1024]{2,1,0:T(8,128)}, u32[]{:S(2)}) copy-start(f32[2,32,1024]{2,1,0:T(8,128)} %get-tuple-element.5) | copy-start | bytes 786436

commit v5 on v4

--- a/solution.py
+++ b/solution.py
@@ -260,14 +260,12 @@
         base[g, half:] = old[half:] - (real * start[half:] + imag * start[:half])
 
     def apply(step, sub, k, g):
-        def local(t, carry):
+        images = []
+        for t in range(tiles.shape[0]):
             chosen = jnp.concatenate([field[g, columns[n, t]] for n in range(per_row)], axis=1)
             stored = tiles[t].reshape(per_row * tile, tile)
-            lanes = pl.ds(pl.multiple_of(t * tile, tile), tile)
-            residual[g, :, lanes] = base[g, :, lanes] - fold(dot(chosen, stored))
-            return carry
-
-        lax.fori_loop(0, tiles.shape[0], local, 0, unroll=2)
+            images.append(fold(dot(chosen, stored)))
+        residual[g] = base[g] - jnp.concatenate(images, axis=1)
 
         result = residual[g]
         for first in range(directions - 2, -1, -2):
@@ -359,6 +357,19 @@
     each_group(finish)
     for store in stores:
         store.wait()
+
+
+def hand_over(first, second, first_out, second_out, sem):
+    copies = []
+    for place, (source, target) in enumerate([(first, first_out), (second, second_out)]):
+        for p in range(source.shape[0]):
+            copies.append(
+                pltpu.make_async_copy(source.at[p], target.at[p], sem.at[place, p])
+            )
+    for copy in copies:
+        copy.start()
+    for copy in copies:
+        copy.wait()
 
 
 def on_device(
@@ -436,6 +447,14 @@
         local_modes[0, 0],
         inverse,
     )
+    results = pl.pallas_call(
+        hand_over,
+        out_shape=(flat, flat),
+        in_specs=[hbm, hbm],
+        out_specs=(hbm, hbm),
+        scratch_shapes=[pltpu.SemaphoreType.DMA((2, shape[2]))],
+        compiler_params=pltpu.CompilerParams(vmem_limit_bytes=63 * 1024 * 1024),
+    )(*results)
     return tuple(value.reshape(shape) for value in results)
 
 

time: 55.3 us -> 69 us (1.25)
  Pallas kernels: 51.6 us -> 68.2 us
  local copies, waits for them, and re-layouts: 2.42 us -> 0 us
    pallas_call x0 -> x1, Pallas kernels: none -> 17 us  [on_device(): pl.pallas_call(hand_over, out_shape=(flat, flat), in_specs=[hbm, hbm], ou...]
    unnamed x4 -> x0, local copies, waits for them, and re-layouts: 2.42 us -> none
where the time goes in v5:
time: 69 us; the launch traced here: 68.8 us
  Pallas kernels  68.2 us (99%)
    pallas_call x1, Pallas kernels, on_device(): pl.pallas_call(functools.partial(kernel, n_row, n_col), out_shape=(flat,...  51.2 us
    pallas_call x1, Pallas kernels, on_device(): pl.pallas_call(hand_over, out_shape=(flat, flat), in_specs=[hbm, hbm], ou...  17 us

profile of v5, /device:TPU:0, one launch (start us, length us, event | category | flops | bytes accessed | tf_op | source)
XLA Modules:
  0.0 68.8 jit_solution(10909162347029788659)
XLA Ops:
  0.6 51.2 %shard_map.113 = (f32[2,32,1024]{2,1,0:T(8,128)}, f32[2,32,1024]{2,1,0:T(8,128)}) custom-call(s32[4,8]{1,0:T(4,128)} %bitcast.21, s32[4,128]{1,0:T(4,128)} %bitcast.22, s32[4,128]{1,0:T(4,128)} %bitcast.23, f32[1,1024]{1,0:T(1,128)} %bitcast.19, f32[1,1024]{1,0:T(1,128)} %bitcast.20, f32[2,32,1024]{2,1,0:T(8,128)} %bitcast.16, ...), custom_call_target="tpu_custom_call" | custom-call | tf_op jit(solution)/shard_map/pallas_call | solution.py:403
  51.8 17.0 %shard_map.114 = (f32[2,32,1024]{2,1,0:T(8,128)}, f32[2,32,1024]{2,1,0:T(8,128)}) custom-call(f32[2,32,1024]{2,1,0:T(8,128)} %get-tuple-element.6.first, f32[2,32,1024]{2,1,0:T(8,128)} %get-tuple-element.7.second), custom_call_target="tpu_custom_call" | custom-call | tf_op jit(solution)/shard_map/pallas_call | solution.py:450

commit v6 on v5

--- a/solution.py
+++ b/solution.py
@@ -9,7 +9,7 @@
 
 OUTER = 2
 PASSES = 2
-GROUPS = 2
+GROUPS = 1
 MESH = pl.DeviceIdType.MESH
 NT = (((1,), (1,)), ((), ()))
 NN = (((1,), (0,)), ((), ()))
@@ -359,17 +359,24 @@
         store.wait()
 
 
-def hand_over(first, second, first_out, second_out, sem):
-    copies = []
+def hand_over(first, second, first_out, second_out, held, arrive_sem, leave_sem):
+    arrivals, departures = [], []
     for place, (source, target) in enumerate([(first, first_out), (second, second_out)]):
         for p in range(source.shape[0]):
-            copies.append(
-                pltpu.make_async_copy(source.at[p], target.at[p], sem.at[place, p])
+            slot = held.at[place, p]
+            arrivals.append(
+                pltpu.make_async_copy(source.at[p], slot, arrive_sem.at[place, p])
             )
-    for copy in copies:
-        copy.start()
-    for copy in copies:
-        copy.wait()
+            departures.append(
+                pltpu.make_async_copy(slot, target.at[p], leave_sem.at[place, p])
+            )
+    for arrival in arrivals:
+        arrival.start()
+    for arrival, departure in zip(arrivals, departures):
+        arrival.wait()
+        departure.start()
+    for departure in departures:
+        departure.wait()
 
 
 def on_device(
@@ -452,7 +459,11 @@
         out_shape=(flat, flat),
         in_specs=[hbm, hbm],
         out_specs=(hbm, hbm),
-        scratch_shapes=[pltpu.SemaphoreType.DMA((2, shape[2]))],
+        scratch_shapes=[
+            pltpu.VMEM((2,) + shape[2:], jnp.float32),
+            pltpu.SemaphoreType.DMA((2, shape[2])),
+            pltpu.SemaphoreType.DMA((2, shape[2])),
+        ],
         compiler_params=pltpu.CompilerParams(vmem_limit_bytes=63 * 1024 * 1024),
     )(*results)
     return tuple(value.reshape(shape) for value in results)

time: 69 us -> 55.9 us (0.81)
  Pallas kernels: 68.2 us -> 55 us
    pallas_call x1, Pallas kernels: 17 us -> 1.82 us  [on_device(): pl.pallas_call(hand_over, out_shape=(flat, flat), in_specs=[hbm, hbm], ou...]
    pallas_call x1, Pallas kernels: 51.2 us -> 53.2 us  [on_device(): pl.pallas_call(functools.partial(kernel, n_row, n_col), out_shape=(flat,...]
where the time goes in v6:
time: 55.9 us; the launch traced here: 55.7 us
  Pallas kernels  55 us (98%)
  between operations  0.64 us (1%)
    pallas_call x1, Pallas kernels, on_device(): pl.pallas_call(functools.partial(kernel, n_row, n_col), out_shape=(flat,...  53.2 us
    pallas_call x1, Pallas kernels, on_device(): pl.pallas_call(hand_over, out_shape=(flat, flat), in_specs=[hbm, hbm], ou...  1.82 us

profile of v6, /device:TPU:0, one launch (start us, length us, event | category | flops | bytes accessed | tf_op | source)
XLA Modules:
  0.0 55.7 jit_solution(16261080782965415290)
XLA Ops:
  0.6 53.2 %shard_map.113 = (f32[2,32,1024]{2,1,0:T(8,128)}, f32[2,32,1024]{2,1,0:T(8,128)}) custom-call(s32[4,8]{1,0:T(4,128)} %bitcast.21, s32[4,128]{1,0:T(4,128)} %bitcast.22, s32[4,128]{1,0:T(4,128)} %bitcast.23, f32[1,1024]{1,0:T(1,128)} %bitcast.19, f32[1,1024]{1,0:T(1,128)} %bitcast.20, f32[2,32,1024]{2,1,0:T(8,128)} %bitcast.16, ...), custom_call_target="tpu_custom_call" | custom-call | tf_op jit(solution)/shard_map/pallas_call | solution.py:410
  53.8 1.8 %shard_map.114 = (f32[2,32,1024]{2,1,0:T(8,128)}, f32[2,32,1024]{2,1,0:T(8,128)}) custom-call(f32[2,32,1024]{2,1,0:T(8,128)} %get-tuple-element.6.first, f32[2,32,1024]{2,1,0:T(8,128)} %get-tuple-element.7.second), custom_call_target="tpu_custom_call" | custom-call | tf_op jit(solution)/shard_map/pallas_call | solution.py:457

commit v7 on v6

--- a/solution.py
+++ b/solution.py
@@ -9,7 +9,7 @@
 
 OUTER = 2
 PASSES = 2
-GROUPS = 1
+GROUPS = 2
 MESH = pl.DeviceIdType.MESH
 NT = (((1,), (1,)), ((), ()))
 NN = (((1,), (0,)), ((), ()))

time: 55.9 us -> 53.8 us (0.962)
  Pallas kernels: 55 us -> 53 us
    pallas_call x1, Pallas kernels: 53.2 us -> 51.2 us  [on_device(): pl.pallas_call(functools.partial(kernel, n_row, n_col), out_shape=(flat,...]
where the time goes in v7:
time: 53.8 us; the launch traced here: 53.6 us
  Pallas kernels  53 us (99%)
  between operations  0.64 us (1%)
    pallas_call x1, Pallas kernels, on_device(): pl.pallas_call(functools.partial(kernel, n_row, n_col), out_shape=(flat,...  51.2 us
    pallas_call x1, Pallas kernels, on_device(): pl.pallas_call(hand_over, out_shape=(flat, flat), in_specs=[hbm, hbm], ou...  1.82 us

profile of v7, /device:TPU:0, one launch (start us, length us, event | category | flops | bytes accessed | tf_op | source)
XLA Modules:
  0.0 53.6 jit_solution(7047410318270970181)
XLA Ops:
  0.6 51.2 %shard_map.113 = (f32[2,32,1024]{2,1,0:T(8,128)}, f32[2,32,1024]{2,1,0:T(8,128)}) custom-call(s32[4,8]{1,0:T(4,128)} %bitcast.21, s32[4,128]{1,0:T(4,128)} %bitcast.22, s32[4,128]{1,0:T(4,128)} %bitcast.23, f32[1,1024]{1,0:T(1,128)} %bitcast.19, f32[1,1024]{1,0:T(1,128)} %bitcast.20, f32[2,32,1024]{2,1,0:T(8,128)} %bitcast.16, ...), custom_call_target="tpu_custom_call" | custom-call | tf_op jit(solution)/shard_map/pallas_call | solution.py:410
  51.8 1.8 %shard_map.114 = (f32[2,32,1024]{2,1,0:T(8,128)}, f32[2,32,1024]{2,1,0:T(8,128)}) custom-call(f32[2,32,1024]{2,1,0:T(8,128)} %get-tuple-element.6.first, f32[2,32,1024]{2,1,0:T(8,128)} %get-tuple-element.7.second), custom_call_target="tpu_custom_call" | custom-call | tf_op jit(solution)/shard_map/pallas_call | solution.py:457
